TPU v7x, 32 devices: a whole 2x2x4 slice. The times are simulated.
32 devices in a mesh: dp: 16 (over z, x, core), tensor: 2 (over y).
Axes of the slice: x: 2, y: 2, z: 4, core: 2. Of those that a mesh axis runs over, the one named last changes fastest.
Arguments:
- inputs: bfloat16 [3152, 768], P('dp'), may hold values from -6 to 6
- cotangent: bfloat16 [3152, 768], P('dp'), may hold values from -6 to 6
- mixing_weight: bfloat16 [3, 768, 768], P(None, 'dp', 'tensor'), may hold values from -0.21875 to 0.21875
- output_weight: bfloat16 [768, 768], P('tensor', 'dp'), may hold values from -0.875 to 0.875
- up_weight: bfloat16 [768, 3072], P('dp', 'tensor'), may hold values from -0.21875 to 0.21875
- down_weight: bfloat16 [3072, 768], P('tensor', 'dp'), may hold values from -0.109375 to 0.109375
- first_gain: float32 [768], replicated, may hold values from 0.5 to 1.5
- first_shift: float32 [768], replicated, may hold values from -3 to 3
- attend_bias: float32 [2, 768], P(None, 'tensor'), may hold values from -3 to 3
- output_bias: float32 [768], replicated, may hold values from -3 to 3
- hidden_bias: float32 [3072], P('tensor'), may hold values from -3 to 3
- final_bias: float32 [768], replicated, may hold values from -3 to 3
- second_gain: float32 [768], replicated, may hold values from 0.5 to 1.5
- second_shift: float32 [768], replicated, may hold values from -3 to 3
Outputs:
- layer_output: bfloat16 [3152, 768], P('dp')
- input_grad: bfloat16 [3152, 768], P('dp')
- mixing_grad: float32 [3, 768, 768], P(None, 'dp', 'tensor')
- outweight_grad: float32 [768, 768], P('tensor', 'dp')
- upweight_grad: float32 [768, 3072], P('dp', 'tensor')
- downweight_grad: float32 [3072, 768], P('tensor', 'dp')
- firstgain_grad: float32 [768], replicated
- firstshift_grad: float32 [768], replicated
- attendbias_grad: float32 [2, 768], P(None, 'tensor')
- outbias_grad: float32 [768], replicated
- hiddenbias_grad: float32 [3072], P('tensor')
- finalbias_grad: float32 [768], replicated
- secondgain_grad: float32 [768], replicated
- secondshift_grad: float32 [768], replicated
All inputs are finite; a program needn't handle non-finite values.
Results may differ from a plain program's by a relative error of at most 0.011.
Values may be sent and summed in bfloat16 or wider, within the bound.
A program may use at most 128 MiB of HBM per device.

v0:
```python
import jax
import jax.numpy as jnp
from jax import lax
from jax.sharding import PartitionSpec as P

HD = 64
SEQ = 197


EPSILON = 1e-06


def norm_forward(values, gain, shift):
    center = values - jnp.mean(values, axis=-1, keepdims=True)
    inverse = lax.rsqrt(jnp.mean(center * center, axis=-1, keepdims=True) + EPSILON)
    normed = center * inverse
    return (normed, inverse, normed * gain + shift)


def norm_backward(upstream, normed, inverse, gain):
    scaled = upstream * gain
    return inverse * (
        scaled
        - jnp.mean(scaled, axis=-1, keepdims=True)
        - normed * jnp.mean(scaled * normed, axis=-1, keepdims=True)
    )


def gelu_pair(values):
    normal_cdf = 0.5 * (1.0 + lax.erf(values * 0.7071067811865476))
    density = 0.3989422804014327 * jnp.exp(-0.5 * values * values)
    return (values * normal_cdf, normal_cdf + values * density)


def matmul(left, right):
    return jnp.dot(left, right, preferred_element_type=jnp.float32)


def local(
    inputs,
    cotangent,
    mixing_weight,
    output_weight,
    up_weight,
    down_weight,
    first_gain,
    first_shift,
    attend_bias,
    output_bias,
    hidden_bias,
    final_bias,
    second_gain,
    second_shift,
):
    mixing_full, output_full, up_full, down_full = (
        lax.all_gather(mixing_weight, "dp", axis=1, tiled=True),
        lax.all_gather(output_weight, "dp", axis=1, tiled=True),
        lax.all_gather(up_weight, "dp", axis=0, tiled=True),
        lax.all_gather(down_weight, "dp", axis=1, tiled=True),
    )
    row_count = inputs.shape[0]
    images = row_count // SEQ
    width = mixing_full.shape[2]
    split_shape = (images, SEQ, width // HD, HD)
    scale = HD ** (-0.5)
    source = inputs.astype(jnp.float32)
    normed_one, inverse_one, affine_one = norm_forward(source, first_gain, first_shift)
    mixed_in = affine_one.astype(jnp.bfloat16)
    projected = jnp.einsum("nd,jde->jne", mixed_in, mixing_full, preferred_element_type=jnp.float32)
    query = (projected[0] + attend_bias[0]).astype(jnp.bfloat16).reshape(split_shape)
    keys = projected[1].astype(jnp.bfloat16).reshape(split_shape)
    values = (projected[2] + attend_bias[1]).astype(jnp.bfloat16).reshape(split_shape)
    scores = jnp.einsum("bqhd,bkhd->bhqk", query, keys, preferred_element_type=jnp.float32) * scale
    top = jnp.max(scores, axis=-1, keepdims=True)
    logsum = top + jnp.log(jnp.sum(jnp.exp(scores - top), axis=-1, keepdims=True))
    probs = jnp.exp(scores - logsum).astype(jnp.bfloat16)
    attended = (
        jnp.einsum("bhqk,bkhd->bqhd", probs, values, preferred_element_type=jnp.float32)
        .astype(jnp.bfloat16)
        .reshape(row_count, width)
    )
    residual = source + lax.psum(matmul(attended, output_full), "tensor") + output_bias
    normed_two, inverse_two, affine_two = norm_forward(residual, second_gain, second_shift)
    hidden_in = affine_two.astype(jnp.bfloat16)
    preact = matmul(hidden_in, up_full) + hidden_bias
    active_full, slope = gelu_pair(preact)
    active = active_full.astype(jnp.bfloat16)
    layer_output = (residual + lax.psum(matmul(active, down_full), "tensor") + final_bias).astype(
        jnp.bfloat16
    )
    mixing_back, output_back, up_back, down_back = (mixing_full, output_full, up_full, down_full)
    upstream = cotangent.astype(jnp.float32)
    down_grad = matmul(active.T, cotangent)
    finalbias_grad = jnp.sum(upstream, axis=0)
    pre_grad = matmul(cotangent, down_back.T) * slope
    pre_half = pre_grad.astype(jnp.bfloat16)
    up_grad = matmul(hidden_in.T, pre_half)
    hiddenbias_grad = jnp.sum(pre_grad, axis=0)
    affine_two_grad = lax.psum(matmul(pre_half, up_back.T), "tensor")
    secondgain_grad = jnp.sum(affine_two_grad * normed_two, axis=0)
    secondshift_grad = jnp.sum(affine_two_grad, axis=0)
    residual_grad = upstream + norm_backward(affine_two_grad, normed_two, inverse_two, second_gain)
    residual_half = residual_grad.astype(jnp.bfloat16)
    outweight_grad = matmul(attended.T, residual_half)
    outbias_grad = jnp.sum(residual_grad, axis=0)
    attended_grad = matmul(residual_half, output_back.T).astype(jnp.bfloat16).reshape(split_shape)
    recomputed = (
        jnp.einsum("bqhd,bkhd->bhqk", query, keys, preferred_element_type=jnp.float32) * scale
    )
    probs_full = jnp.exp(recomputed - logsum)
    prob_grad = jnp.einsum(
        "bqhd,bkhd->bhqk", attended_grad, values, preferred_element_type=jnp.float32
    )
    delta = jnp.sum(probs_full * prob_grad, axis=-1, keepdims=True)
    score_grad = (probs_full * (prob_grad - delta) * scale).astype(jnp.bfloat16)
    query_grad = jnp.einsum(
        "bhqk,bkhd->bqhd", score_grad, keys, preferred_element_type=jnp.float32
    ).reshape(row_count, width)
    keys_grad = jnp.einsum(
        "bhqk,bqhd->bkhd", score_grad, query, preferred_element_type=jnp.float32
    ).reshape(row_count, width)
    values_grad = jnp.einsum(
        "bhqk,bqhd->bkhd", probs, attended_grad, preferred_element_type=jnp.float32
    ).reshape(row_count, width)
    attendbias_grad = jnp.stack([jnp.sum(query_grad, axis=0), jnp.sum(values_grad, axis=0)])
    stacked = jnp.stack([query_grad, keys_grad, values_grad]).astype(jnp.bfloat16)
    mixing_grad = jnp.einsum("nd,jne->jde", mixed_in, stacked, preferred_element_type=jnp.float32)
    affine_one_grad = lax.psum(
        jnp.einsum("jne,jde->nd", stacked, mixing_back, preferred_element_type=jnp.float32),
        "tensor",
    )
    firstgain_grad = jnp.sum(affine_one_grad * normed_one, axis=0)
    firstshift_grad = jnp.sum(affine_one_grad, axis=0)
    input_grad = (
        residual_grad + norm_backward(affine_one_grad, normed_one, inverse_one, first_gain)
    ).astype(jnp.bfloat16)
    mixing_share, output_share, up_share, down_share = (
        lax.psum_scatter(mixing_grad, "dp", scatter_dimension=1, tiled=True),
        lax.psum_scatter(outweight_grad, "dp", scatter_dimension=1, tiled=True),
        lax.psum_scatter(up_grad, "dp", scatter_dimension=0, tiled=True),
        lax.psum_scatter(down_grad, "dp", scatter_dimension=1, tiled=True),
    )
    vector_totals = lax.psum(
        (
            firstgain_grad,
            firstshift_grad,
            attendbias_grad,
            outbias_grad,
            hiddenbias_grad,
            finalbias_grad,
            secondgain_grad,
            secondshift_grad,
        ),
        "dp",
    )
    return (
        layer_output,
        input_grad,
        mixing_share,
        output_share,
        up_share,
        down_share,
        vector_totals[0],
        vector_totals[1],
        vector_totals[2],
        vector_totals[3],
        vector_totals[4],
        vector_totals[5],
        vector_totals[6],
        vector_totals[7],
    )


def solution(mesh):
    placed = (
        P("dp", None),
        P("dp", None),
        P(None, "dp", "tensor"),
        P("tensor", "dp"),
        P("dp", "tensor"),
        P("tensor", "dp"),
        P(),
        P(),
        P(None, "tensor"),
        P(),
        P("tensor"),
        P(),
        P(),
        P(),
    )
    return jax.shard_map(
        local,
        mesh=mesh,
        in_specs=placed,
        out_specs=(
            P("dp", None),
            P("dp", None),
            P(None, "dp", "tensor"),
            P("tensor", "dp"),
            P("dp", "tensor"),
            P("tensor", "dp"),
            P(),
            P(),
            P(None, "tensor"),
            P(),
            P("tensor"),
            P(),
            P(),
            P(),
        ),
        check_vma=False,
    )
```

profile of v0, /device:TPU:0, one launch (start us, length us, event | category | flops | bytes accessed | tf_op | source)
XLA Modules:
  0.0 626.8 jit_solution(11460762559043077336)
XLA Ops:
  7.3 0.7 all-gather.4.cloned.1.call-update
  8.0 0.8 slice_reduce_fusion.1
  8.9 1.1 convert_reduce_fusion
  10.0 1.2 fusion.29
  11.3 25.7 %all_gather.13 = bf16[384,768]{0,1:T(8,128)(2,1)S(1)} all-gather(bf16[384,48]{0,1:T(8,128)(2,1)} %param.17), channel_id=1, replica_groups=mesh['dp'=16,'tensor'=2] {'dp'}, dimensions={1}, use_global_device_ids=true | all-gather | bytes 626688 | tf_op jit(solution)/shard_map/all_gather | solution.py:57
  37.0 17.6 %all-gather.4.cloned.1.call-done = bf16[3,768,384]{2,1,0:T(8,128)(2,1)} async-done(((bf16[3,48,384]{2,1,0:T(8,128)(2,1)}), bf16[3,768,384]{2,1,0:T(8,128)(2,1)}) %all-gather.4.cloned.1.call-update) | async-done | bytes 1769488 | tf_op jit(solution)/shard_map/all_gather | solution.py:56
  54.6 2.1 convolution_bitcast_fusion.1
  58.5 1.2 fusion.66
  59.8 0.7 all-gather.6.cloned.1.call-update
  61.1 28.3 %all-reduce.8.cloned.1.call-done = f32[197,768]{1,0:T(8,128)} async-done(((f32[197,768]{1,0:T(8,128)}), f32[197,768]{1,0:T(8,128)}) %all-reduce.8.cloned.1.call-update) | async-done | bytes 605200 | tf_op jit(solution)/shard_map/psum | solution.py:82
  89.4 1.2 fusion.57
  92.0 42.2 %all-gather.6.cloned.1.call-done = bf16[768,1536]{1,0:T(8,128)(2,1)} async-done(((bf16[48,1536]{1,0:T(8,128)(2,1)}), bf16[768,1536]{1,0:T(8,128)(2,1)}) %all-gather.6.cloned.1.call-update) | async-done | bytes 2359312 | tf_op jit(solution)/shard_map/all_gather | solution.py:58
  134.2 3.5 multiply_convert_fusion
  137.7 39.7 %all-gather.8.cloned.1.call-done = bf16[1536,768]{0,1:T(8,128)(2,1)} async-done(((bf16[1536,48]{0,1:T(8,128)(2,1)}), bf16[1536,768]{0,1:T(8,128)(2,1)}) %all-gather.8.cloned.1.call-update) | async-done | bytes 2359312 | tf_op jit(solution)/shard_map/all_gather | solution.py:59
  177.5 3.7 fusion.65
  181.2 0.8 copy-done.7
  182.0 1.7 fusion.40
  183.8 3.4 fusion.67
  187.1 26.1 %all-reduce.10.cloned.1.call-done = f32[197,768]{1,0:T(8,128)} async-done(((f32[197,768]{1,0:T(8,128)}), f32[197,768]{1,0:T(8,128)}) %all-reduce.10.cloned.1.call-update) | async-done | bytes 605200 | tf_op jit(solution)/shard_map/psum | solution.py:99
  213.2 2.2 multiply_reduce_fusion.1
  215.4 0.9 fusion.56
  216.3 1.0 convolution_convert_fusion.2
  217.3 1.1 copy.58
  218.5 2.3 fusion.61
  220.8 1.5 fusion.49
  222.3 3.2 convolution_convert_fusion
  225.5 3.1 fusion.60
  228.8 1.1 copy.63
  229.9 3.1 convolution_bitcast_fusion.2
  233.1 0.6 copy-done.20
  233.7 2.6 convolution_bitcast_fusion
  236.3 6.3 %copy.65 = f32[3,768,384]{2,0,1:T(4,128)} copy(f32[3,768,384]{1,2,0:T(8,128)} %convolution_bitcast_fusion) | data formatting | bytes 7077888 | tf_op jit(solution)/shard_map/nd,jne->jde/transpose | solution.py:127
  242.7 1.5 fusion.44
  244.5 3.2 fusion.38
  247.8 1.0 copy-done.2
  248.9 3.0 fusion.68
  252.5 0.6 dynamic-slice
  253.9 23.6 %all-reduce.14.cloned.1.call-done = (f32[197,768]{1,0:T(8,128)}, f32[197,768]{1,0:T(8,128)}) async-done(((f32[197,768]{1,0:T(8,128)}, f32[197,768]{1,0:T(8,128)}), (f32[197,768]{1,0:T(8,128)}, f32[197,768]{1,0:T(8,128)})) %all-reduce.14.cloned.1.call-update) | async-done | bytes 1210384 | tf_op jit(solution)/shard_map/psum | solution.py:88
  277.5 1.6 fusion.28
  279.1 63.5 %all-reduce.1 = (f32[768]{0:T(1024)}, f32[768]{0:T(1024)}, f32[2,384]{1,0:T(2,128)}, f32[768]{0:T(1024)}, f32[1536]{0:T(1024)}, /*index=5*/f32[768]{0:T(1024)}, f32[768]{0:T(1024)}, f32[768]{0:T(1024)}) all-reduce(f32[768]{0:T(1024)S(1)} %get-tuple-element.58, ...), channel_id=1, replica_groups=mesh['dp'=16,'tensor'=2] {'dp'}, use_global_device_ids=true, to_apply=%region_20.0 | all-reduce | flops 6912 | bytes 55296 | tf_op jit(solution)/shard_map/psum | solution.py:143
  342.6 0.8 add_convert_fusion
  343.4 1.0 fusion.27
  344.4 54.7 %all-reduce.12.cloned.1.call-done = f32[3,768,384]{2,0,1:T(4,128)} async-done(((f32[3,768,384]{2,0,1:T(4,128)}), f32[3,768,384]{2,0,1:T(4,128)}) %all-reduce.12.cloned.1.call-update) | async-done | bytes 3538960
  399.1 1.0 constant_dynamic-slice_fusion
  400.1 0.7 copy.66
  400.8 60.7 %reduce-scatter.4.cloned.1.call-done = f32[384,48]{0,1:T(8,128)} async-done(((f32[384,768]{0,1:T(8,128)}), f32[384,48]{0,1:T(8,128)}) %reduce-scatter.4.cloned.1.call-update) | async-done | bytes 73744 | tf_op jit(solution)/shard_map/reduce_scatter | solution.py:139
  461.5 79.5 %reduce-scatter.6.cloned.1.call-done = f32[48,1536]{1,0:T(8,128)} async-done(((f32[768,1536]{1,0:T(8,128)}), f32[48,1536]{1,0:T(8,128)}) %reduce-scatter.6.cloned.1.call-update) | async-done | bytes 294928 | tf_op jit(solution)/shard_map/reduce_scatter | solution.py:140
  541.0 78.9 %reduce-scatter.8.cloned.1.call-done = f32[1536,48]{0,1:T(8,128)} async-done(((f32[1536,768]{0,1:T(8,128)}), f32[1536,48]{0,1:T(8,128)}) %reduce-scatter.8.cloned.1.call-update) | async-done | bytes 294928 | tf_op jit(solution)/shard_map/reduce_scatter | solution.py:141
  (131 shorter events, 5.6 us)
Async XLA Ops:
  7.2 47.4 %copy-start = (bf16[197,768]{1,0:T(8,128)(2,1)S(1)}, bf16[197,768]{1,0:T(8,128)(2,1)}, u32[]{:S(2)}) copy-start(bf16[197,768]{1,0:T(8,128)(2,1)} %param.14) | copy-start | bytes 907780
  7.2 47.4 %copy-start.18 = (f32[768]{0:T(1024)S(1)}, f32[768]{0:T(1024)}, u32[]{:S(2)}) copy-start(f32[768]{0:T(1024)} %param.20) | copy-start | bytes 9220
  7.2 47.4 %copy-start.36 = (f32[768]{0:T(1024)S(1)}, f32[768]{0:T(1024)}, u32[]{:S(2)}) copy-start(f32[768]{0:T(1024)} %param.21) | copy-start | bytes 9220
  7.2 47.4 %all-gather.4.cloned.1.call-start = ((), (), s32[]{:S(2)}) async-start(), calls=%async_computation.3 | async-start | bytes 1880064 | tf_op jit(solution)/shard_map/all_gather | solution.py:56
  7.9 81.4 %all-reduce.8.cloned.1.call-start = ((), (), s32[]{:S(2)}) async-start(), calls=%async_computation.4 | async-start | bytes 1228800 | tf_op jit(solution)/shard_map/psum | solution.py:82
  8.9 49.2 %copy-start.21 = (f32[6,64]{1,0:T(8,128)}, f32[6,64]{1,0:T(8,128)S(1)}, u32[]{:S(2)}) copy-start(f32[6,64]{1,0:T(8,128)S(1)} %add.146) | copy-start | bytes 4612
  8.9 48.4 %copy-start.34 = (f32[6,64]{1,0:T(8,128)}, f32[6,64]{1,0:T(8,128)S(1)}, u32[]{:S(2)}) copy-start(f32[6,64]{1,0:T(8,128)S(1)} %add.149) | copy-start | bytes 4612
  10.0 46.7 %copy-start.19 = (f32[197]{0:T(256)}, f32[197]{0:T(256)S(1)}, u32[]{:S(2)}) copy-start(f32[197]{0:T(256)S(1)} %broadcast_multiply_fusion.5) | copy-start | bytes 2368
  11.3 45.5 %copy-start.25 = (f32[197]{0:T(256)}, f32[197]{0:T(256)S(1)}, u32[]{:S(2)}) copy-start(f32[197]{0:T(256)S(1)} %add_rsqrt_fusion.1) | copy-start | bytes 2368
  57.1 1.0 copy-start.3
  58.1 1.6 copy-start.17
  58.5 30.9 %copy-start.41 = (f32[768]{0:T(1024)S(1)}, f32[768]{0:T(1024)}, u32[]{:S(2)}) copy-start(f32[768]{0:T(1024)} %param.23) | copy-start | bytes 9220
  59.7 74.4 %all-gather.6.cloned.1.call-start = ((), (), s32[]{:S(2)}) async-start(), calls=%async_computation.5 | async-start | bytes 2506752 | tf_op jit(solution)/shard_map/all_gather | solution.py:58
  60.5 117.0 %all-gather.8.cloned.1.call-start = ((), (), s32[]{:S(2)}) async-start(), calls=%async_computation.6 | async-start | bytes 2506752 | tf_op jit(solution)/shard_map/all_gather | solution.py:59
  61.0 152.2 %all-reduce.10.cloned.1.call-start = ((), (), s32[]{:S(2)}) async-start(), calls=%async_computation.7 | async-start | bytes 1228800 | tf_op jit(solution)/shard_map/psum | solution.py:99
  137.7 46.0 %copy-start.1 = (bf16[197,1536]{1,0:T(8,128)(2,1)}, bf16[197,1536]{1,0:T(8,128)(2,1)S(1)}, u32[]{:S(2)}) copy-start(bf16[197,1536]{1,0:T(8,128)(2,1)S(1)} %get-tuple-element.89) | copy-start | bytes 1815556
  177.5 4.5 copy-start.9
  183.7 93.8 %all-reduce.14.cloned.1.call-start = ((), (), s32[]{:S(2)}) async-start(), calls=%async_computation.12 | async-start | bytes 2457600 | tf_op jit(solution)/shard_map/psum | solution.py:88
  213.2 2.2 copy-start.6
  213.2 2.2 copy-start.11
  213.2 2.2 copy-start.23
  213.2 2.2 copy-start.28
  213.2 2.2 copy-start.38
  217.3 3.4 copy-start.4
  218.4 2.3 copy-start.22
  222.3 3.2 copy-start.14
  225.5 3.1 copy-start.15
  233.0 166.1 %all-reduce.12.cloned.1.call-start = ((), (), s32[]{:S(2)}) async-start(), calls=%async_computation.11 | async-start | bytes 9437184
  242.6 1.8 copy-start.8
  242.6 1.8 copy-start.24
  242.6 1.8 copy-start.29
  242.7 1.8 copy-start.39
  242.7 1.8 copy-start.44
  242.7 218.8 %reduce-scatter.4.cloned.1.call-start = ((), (), s32[]{:S(2)}) async-start(), calls=%async_computation.8 | async-start | bytes 1253376 | tf_op jit(solution)/shard_map/reduce_scatter | solution.py:139
  244.2 296.8 %reduce-scatter.6.cloned.1.call-start = ((), (), s32[]{:S(2)}) async-start(), calls=%async_computation.9 | async-start | bytes 5013504 | tf_op jit(solution)/shard_map/reduce_scatter | solution.py:140
  247.7 1.1 copy-start.2
  247.7 1.2 copy-start.12
  247.7 372.2 %reduce-scatter.8.cloned.1.call-start = ((), (), s32[]{:S(2)}) async-start(), calls=%async_computation.10 | async-start | bytes 5013504 | tf_op jit(solution)/shard_map/reduce_scatter | solution.py:141
  251.8 1.9 copy-start.35
  251.8 2.0 copy-start.43
  251.8 27.3 %copy-start.30 = (f32[768]{0:T(1024)S(1)}, f32[768]{0:T(1024)}, u32[]{:S(2)}) copy-start(f32[768]{0:T(1024)} %get-tuple-element.56) | copy-start | bytes 9220
  251.8 27.3 %copy-start.31 = (f32[768]{0:T(1024)S(1)}, f32[768]{0:T(1024)}, u32[]{:S(2)}) copy-start(f32[768]{0:T(1024)} %get-tuple-element.62) | copy-start | bytes 9220
  251.9 27.3 %copy-start.32 = (f32[768]{0:T(1024)S(1)}, f32[768]{0:T(1024)}, u32[]{:S(2)}) copy-start(f32[768]{0:T(1024)} %get-tuple-element.76) | copy-start | bytes 9220
  251.9 27.2 %copy-start.33 = (f32[768]{0:T(1024)S(1)}, f32[768]{0:T(1024)}, u32[]{:S(2)}) copy-start(f32[768]{0:T(1024)} %get-tuple-element.86) | copy-start | bytes 9220
  251.9 27.2 %copy-start.40 = (f32[1536]{0:T(1024)S(1)}, f32[1536]{0:T(1024)}, u32[]{:S(2)}) copy-start(f32[1536]{0:T(1024)} %get-tuple-element.93) | copy-start | bytes 18436
  251.9 90.7 %copy-start.42 = (f32[768]{0:T(1024)S(1)}, f32[768]{0:T(1024)}, u32[]{:S(2)}) copy-start(f32[768]{0:T(1024)} %param.25) | copy-start | bytes 9220
  277.5 65.1 %copy-start.16 = (f32[197,768]{1,0:T(8,128)S(1)}, f32[197,768]{1,0:T(8,128)}, u32[]{:S(2)}) copy-start(f32[197,768]{1,0:T(8,128)} %get-tuple-element.74) | copy-start | bytes 1815556
  277.5 65.9 %copy-start.5 = (f32[197,768]{1,0:T(8,128)S(1)}, f32[197,768]{1,0:T(8,128)}, u32[]{:S(2)}) copy-start(f32[197,768]{1,0:T(8,128)} %get-tuple-element.75) | copy-start | bytes 1815556
  (8 other events, 5.7 us)
Sparse Core Ops, SparseCore 0:
  10.4 44.1 all-gather.3
  59.9 29.4 all-reduce.7
  91.7 42.4 all-gather.5
  136.3 41.0 all-gather.7
  183.8 29.3 all-reduce.9
  233.1 44.3 all-reduce.13
  281.6 117.4 all-reduce.11
  403.7 57.7 reduce-scatter.3
  466.4 74.5 reduce-scatter.5
  545.3 74.6 reduce-scatter.7
where the time goes:
time: 628 us; the launch traced here: 627 us
  waiting for transfers between devices  453 us (72%)
  blocking collectives  89.2 us (14%)
  matrix products  40.8 us (6%)
  local copies, waits for them, and re-layouts  16.6 us (3%)
  between operations  15.3 us (2%)
  other arithmetic  11 us (2%)
    reduce_scatter x1, waiting for transfers between devices, local(): lax.psum_scatter(up_grad, 'dp', scatter_dimension=0, tiled=True)  79.5 us
    reduce_scatter x1, waiting for transfers between devices, local(): lax.psum_scatter(down_grad, 'dp', scatter_dimension=1, tiled=True)  78.9 us
    psum x1, blocking collectives, local(): lax.psum((firstgain_grad, firstshift_grad, attendbias_grad, outbias_grad,...  63.5 us
    reduce_scatter x1, waiting for transfers between devices, local(): lax.psum_scatter(outweight_grad, 'dp', scatter_dimension=1, tiled=True)  60.7 us
    unnamed x11, waiting for transfers between devices  56.7 us
    all_gather x1, waiting for transfers between devices, local(): lax.all_gather(up_weight, 'dp', axis=0, tiled=True)  42.2 us
    all_gather x1, waiting for transfers between devices, local(): lax.all_gather(down_weight, 'dp', axis=1, tiled=True)  39.7 us
    psum x1, waiting for transfers between devices, local(): lax.psum(matmul(attended, output_full), 'tensor')  28.3 us
  transfers between devices with their start and end apart: 10, of which 10 were waited for; matrix products, arithmetic and copies ran while one was open for 6% of the time, Pallas kernels for 0%

commit v1 on v0

--- a/solution.py
+++ b/solution.py
@@ -1,6 +1,10 @@
+import functools
+
 import jax
 import jax.numpy as jnp
 from jax import lax
+from jax.experimental import pallas as pl
+from jax.experimental.pallas import tpu as pltpu
 from jax.sharding import PartitionSpec as P
 
 HD = 64
@@ -36,7 +40,7 @@
     return jnp.dot(left, right, preferred_element_type=jnp.float32)
 
 
-def local(
+def local_plain(
     inputs,
     cotangent,
     mixing_weight,
@@ -171,6 +175,520 @@
     )
 
 
+ROWS = 256
+SENT = 208
+X = 2
+C = 2
+TILE = 384
+SCALE = HD ** (-0.5)
+F32 = jnp.float32
+BF16 = jnp.bfloat16
+
+
+def nt(left, right):
+    return lax.dot_general(left, right, (((1,), (1,)), ((), ())), preferred_element_type=F32)
+
+
+def tn(left, right):
+    return lax.dot_general(left, right, (((0,), (0,)), ((), ())), preferred_element_type=F32)
+
+
+def cols(tile):
+    return pl.ds(pl.multiple_of(tile * TILE, TILE), TILE)
+
+
+def layer_kernel(
+    Z,
+    copies,
+    x_ref,
+    ct_ref,
+    mix_ref,
+    outw_ref,
+    up_ref,
+    down_ref,
+    fg_ref,
+    fs_ref,
+    ab_ref,
+    ob_ref,
+    hb_ref,
+    fb_ref,
+    sg_ref,
+    ss_ref,
+    lo_ref,
+    ig_ref,
+    gmix_ref,
+    gout_ref,
+    gup_ref,
+    gdown_ref,
+    vec_ref,
+    w0,
+    w1,
+    w2,
+    w3,
+    g0,
+    g1,
+    g2,
+    g3,
+    ga0,
+    ga1,
+    ga2,
+    ga3,
+    gb0,
+    gb1,
+    gb2,
+    gb3,
+    gc0,
+    gc1,
+    gc2,
+    gc3,
+    gd0,
+    gd1,
+    gd2,
+    gd3,
+    ge0,
+    ge1,
+    ge2,
+    ge3,
+    ysend,
+    yrecv,
+    vs,
+    vr,
+    left_t,
+    n1_s,
+    n2_s,
+    acc,
+    qkv,
+    prob_s,
+    att,
+    attg,
+    stacked,
+    active,
+    slope,
+    pre_half,
+    a2_s,
+    res_s,
+    rg_s,
+    send_sem,
+    recv_sem,
+):
+    dp = lax.axis_index("dp")
+    tensor = lax.axis_index("tensor")
+    c = lax.rem(dp, C)
+    x = lax.rem(dp // C, X)
+    z = dp // (C * X)
+    w = (w0, w1, w2, w3)
+    g = (g0, g1, g2, g3)
+    ga = (ga0, ga1, ga2, ga3)
+    gb = (gb0, gb1, gb2, gb3)
+    gc = (gc0, gc1, gc2, gc3)
+    gd = (gd0, gd1, gd2, gd3)
+    ge = (ge0, ge1, ge2, ge3)
+
+    def index(zz, xx, cc):
+        return (zz * X + xx) * C + cc
+
+    def zat(step):
+        return lax.rem(z + step + Z, Z)
+
+    peers_z = [{"dp": index(zat(d), x, c), "tensor": tensor} for d in range(1, Z)]
+    peer_x = {"dp": index(z, 1 - x, c), "tensor": tensor}
+    peer_c = {"dp": index(z, x, 1 - c), "tensor": tensor}
+    peer_y = {"dp": dp, "tensor": 1 - tensor}
+
+    started = []
+
+    def send(src, dst, device):
+        k = len(started)
+        copy = pltpu.make_async_remote_copy(
+            src_ref=src,
+            dst_ref=dst,
+            send_sem=send_sem.at[k],
+            recv_sem=recv_sem.at[k],
+            device_id=device,
+            device_id_type=pl.DeviceIdType.MESH,
+        )
+        copy.start()
+        started.append(copy)
+        return copy
+
+    yrecv[:, SENT:ROWS, :] = jnp.zeros((4, ROWS - SENT, yrecv.shape[2]), BF16)
+    for j in range(3):
+        w0[z, x, c, :, j * TILE : (j + 1) * TILE] = mix_ref[j]
+    w1[z, x, c] = outw_ref[...]
+    w2[z, x, c] = up_ref[...]
+    w3[z, x, c] = down_ref[...]
+
+    barrier = pltpu.get_barrier_semaphore()
+    everyone = peers_z + [peer_x, peer_c, peer_y]
+    for device in everyone:
+        pl.semaphore_signal(barrier, inc=1, device_id=device, device_id_type=pl.DeviceIdType.MESH)
+    pl.semaphore_wait(barrier, len(everyone))
+
+    by_z, by_x, by_c, by_d = {}, {}, {}, {}
+    for i in range(4):
+        mine = w[i].at[z, x, c]
+        by_x[i, 0] = send(mine, mine, peer_x)
+        for d in range(1, Z):
+            by_z[i, d] = send(mine, mine, peers_z[d - 1])
+        by_c[i, 0] = send(mine, mine, peer_c)
+
+    def pass_on(i):
+        for d in range(1, Z):
+            by_z[i, d].wait_recv()
+            block = w[i].at[zat(-d), x, c]
+            by_x[i, d] = send(block, block, peer_x)
+            by_c[i, d] = send(block, block, peer_c)
+
+    def pass_core(i):
+        for d in range(Z):
+            by_x[i, d].wait_recv()
+            block = w[i].at[zat(-d), 1 - x, c]
+            by_d[i, d] = send(block, block, peer_c)
+
+    def gathered(i):
+        for d in range(Z):
+            by_c[i, d].wait_recv()
+        for d in range(Z):
+            by_d[i, d].wait_recv()
+
+    def weight(i, tile):
+        return w[i][:, :, :, :, cols(tile)].reshape(-1, TILE)
+
+    def exchange(k):
+        return send(ysend.at[k, pl.ds(0, SENT)], yrecv.at[k, pl.ds(0, SENT)], peer_y)
+
+    def exchanged(k):
+        return ysend[k].astype(F32) + yrecv[k].astype(F32)
+
+    def transposed(value):
+        return value.astype(F32).T.astype(BF16)
+
+    source = x_ref[...].astype(F32)
+    n1, r1, affine = norm_forward(source, fg_ref[...], fs_ref[...])
+    n1_s[...] = n1
+    a1 = affine.astype(BF16)
+    left_t[0] = transposed(a1)
+    left_t[1] = transposed(ct_ref[...])
+    vs[...] = jnp.zeros_like(vs)
+    vs[6:7, :] = jnp.sum(ct_ref[...].astype(F32), axis=0, keepdims=True)
+    pass_on(0)
+    pass_core(0)
+    pass_on(1)
+    gathered(0)
+
+    for j in range(3):
+        value = jnp.dot(a1, weight(0, j), preferred_element_type=F32)
+        if j != 1:
+            value = value + ab_ref[j // 2 : j // 2 + 1, :]
+        qkv[:, j * TILE : (j + 1) * TILE] = value.astype(BF16)
+    pass_core(1)
+
+    heads = TILE // HD
+    seen = lax.broadcasted_iota(jnp.int32, (ROWS, ROWS), 1) < SEQ
+
+    def head(ref, part, h):
+        pair = ref[:, part * TILE + (h // 2) * 128 : part * TILE + (h // 2) * 128 + 128]
+        return pair[:, (h % 2) * HD : (h % 2) * HD + HD]
+
+    halves = []
+    for h in range(heads):
+        q, k, v = head(qkv, 0, h), head(qkv, 1, h), head(qkv, 2, h)
+        scores = jnp.where(seen, nt(q, k) * SCALE, -1e30)
+        top = jnp.max(scores, axis=-1, keepdims=True)
+        logsum = top + jnp.log(jnp.sum(jnp.exp(scores - top), axis=-1, keepdims=True))
+        probs = jnp.exp(scores - logsum)
+        prob_s[h] = probs
+        halves.append(jnp.dot(probs.astype(BF16), v, preferred_element_type=F32))
+        if h % 2 == 1:
+            att[:, (h // 2) * 128 : (h // 2) * 128 + 128] = jnp.concatenate(
+                halves[-2:], axis=1
+            ).astype(BF16)
+        if h == 1:
+            pass_on(2)
+    gathered(1)
+    ysend[0] = nt(att[...], weight(1, 0)).astype(BF16)
+    first = exchange(0)
+    pass_core(2)
+    pass_on(3)
+    first.wait_recv()
+    residual = source + exchanged(0) + ob_ref[...]
+    res_s[...] = residual
+    n2, r2, affine = norm_forward(residual, sg_ref[...], ss_ref[...])
+    n2_s[...] = n2
+    a2_s[...] = affine.astype(BF16)
+    left_t[2] = transposed(affine.astype(BF16))
+    gathered(2)
+    tiles = hb_ref.shape[1] // TILE
+
+    def hidden(tile, carry):
+        value = jnp.dot(a2_s[...], weight(2, tile), preferred_element_type=F32)
+        value, steep = gelu_pair(value + hb_ref[:, cols(tile)])
+        active[:, cols(tile)] = value.astype(BF16)
+        slope[:, cols(tile)] = steep
+        return carry
+
+    lax.fori_loop(0, tiles, hidden, 0)
+    pass_core(3)
+    gathered(3)
+
+    acc[...] = jnp.zeros_like(acc)
+
+    def second(tile, carry):
+        acc[...] += nt(active[:, cols(tile)], weight(3, tile))
+        return carry
+
+    lax.fori_loop(0, tiles, second, 0)
+    ysend[1] = acc[...].astype(BF16)
+    out_copy = exchange(1)
+
+    acc[...] = jnp.zeros_like(acc)
+
+    def back(tile, carry):
+        grad = jnp.dot(ct_ref[...], weight(3, tile), preferred_element_type=F32)
+        grad = grad * slope[:, cols(tile)]
+        sums = jnp.sum(grad, axis=0, keepdims=True)
+        slope[0:8, cols(tile)] = jnp.broadcast_to(sums, (8, TILE))
+        half = grad.astype(BF16)
+        pre_half[:, cols(tile)] = half
+        acc[...] += nt(half, weight(2, tile))
+        return carry
+
+    lax.fori_loop(0, tiles, back, 0)
+    ysend[2] = acc[...].astype(BF16)
+    a2_copy = exchange(2)
+    vs[4:5, :] = slope[0:1, 0:768]
+    vs[5:6, :] = slope[0:1, 768:1536]
+
+    by_a, by_b, by_e = {}, {}, {}
+
+    def gradient(i, left, right, count):
+        def one(tile, carry):
+            value = jnp.dot(left_t[left], right[:, cols(tile)], preferred_element_type=F32)
+            g[i][:, :, :, :, cols(tile)] = value.astype(BF16).reshape(Z, X, C, -1, TILE)
+            return carry
+
+        lax.fori_loop(0, count, one, 0)
+        by_a[i] = send(g[i].at[:, :, 1 - c], ga[i], peer_c)
+
+    def sum_core(i):
+        by_a[i].wait_recv()
+        gb[i][...] = (g[i][:, :, c].astype(F32) + ga[i][...].astype(F32)).astype(BF16)
+        by_b[i] = send(gb[i].at[:, 1 - x], gc[i], peer_x)
+
+    def sum_x(i):
+        by_b[i].wait_recv()
+        gd[i][...] = (gb[i][:, x].astype(F32) + gc[i][...].astype(F32)).astype(BF16)
+        for d in range(1, Z):
+            by_e[i, d] = send(gd[i].at[zat(d)], ge[i].at[d], peers_z[d - 1])
+
+    def sum_z(i):
+        total = gd[i][z].astype(F32)
+        for d in range(1, Z):
+            by_e[i, d].wait_recv()
+            total = total + ge[i][d].astype(F32)
+        return total
+
+    gradient(3, 1, active, tiles)
+    gradient(2, 2, pre_half, tiles)
+    sum_core(3)
+    out_copy.wait_recv()
+    lo_ref[...] = (res_s[...] + exchanged(1) + fb_ref[...]).astype(BF16)
+    a2_copy.wait_recv()
+    a2_grad = exchanged(2)
+    vs[7:8, :] = jnp.sum(a2_grad * n2_s[...], axis=0, keepdims=True)
+    vs[8:9, :] = jnp.sum(a2_grad, axis=0, keepdims=True)
+    res_grad = ct_ref[...].astype(F32) + norm_backward(a2_grad, n2_s[...], r2, sg_ref[...])
+    rg_s[...] = res_grad
+    vs[3:4, :] = jnp.sum(res_grad, axis=0, keepdims=True)
+    res_half = res_grad.astype(BF16)
+    left_t[1] = transposed(res_half)
+    sum_core(2)
+    attg[...] = jnp.dot(res_half, weight(1, 0), preferred_element_type=F32).astype(BF16)
+    gradient(1, 1, att, 1)
+    sum_x(3)
+
+    pairs = {}
+    for h in range(heads):
+        q, k, v = head(qkv, 0, h), head(qkv, 1, h), head(qkv, 2, h)
+        upper = head(attg, 0, h)
+        probs = prob_s[h]
+        prob_grad = nt(upper, v)
+        delta = jnp.sum(probs * prob_grad, axis=-1, keepdims=True)
+        score_grad = (probs * (prob_grad - delta) * SCALE).astype(BF16)
+        pairs[0, h] = jnp.dot(score_grad, k, preferred_element_type=F32)
+        pairs[1, h] = tn(score_grad, q)
+        pairs[2, h] = tn(probs.astype(BF16), upper)
+        if h % 2 == 1:
+            start = (h // 2) * 128
+            for j in range(3):
+                pair = jnp.concatenate([pairs[j, h - 1], pairs[j, h]], axis=1)
+                stacked[:, j * TILE + start : j * TILE + start + 128] = pair.astype(BF16)
+                if j != 1:
+                    place = (j // 2) * TILE + start
+                    vs[2:3, place : place + 128] = jnp.sum(pair, axis=0, keepdims=True)
+        if h == 1:
+            sum_core(1)
+        if h == 3:
+            sum_x(2)
+    total = nt(stacked[:, 0:TILE], weight(0, 0))
+    for j in range(1, 3):
+        total = total + nt(stacked[:, j * TILE : (j + 1) * TILE], weight(0, j))
+    ysend[3] = total.astype(BF16)
+    last = exchange(3)
+    gradient(0, 0, stacked, 3)
+    sum_x(1)
+    last.wait_recv()
+    a1_grad = exchanged(3)
+    vs[0:1, :] = jnp.sum(a1_grad * n1_s[...], axis=0, keepdims=True)
+    vs[1:2, :] = jnp.sum(a1_grad, axis=0, keepdims=True)
+    vec_c = send(vs, vr.at[0], peer_c)
+    sum_core(0)
+    ig_ref[...] = (rg_s[...] + norm_backward(a1_grad, n1_s[...], r1, fg_ref[...])).astype(BF16)
+    vec_c.wait_recv()
+    vr[1] = vs[...] + vr[0]
+    vec_x = send(vr.at[1], vr.at[2], peer_x)
+    gdown_ref[...] = sum_z(3)
+    gup_ref[...] = sum_z(2)
+    vec_x.wait_recv()
+    mine = vr[1] + vr[2]
+    vr[3 + z] = mine
+    vec_z = [send(vr.at[3 + z], vr.at[3 + z], peers_z[d - 1]) for d in range(1, Z)]
+    sum_x(0)
+    gout_ref[...] = sum_z(1)
+    for copy in vec_z:
+        copy.wait_recv()
+    total = vr[3]
+    for d in range(1, Z):
+        total = total + vr[3 + d]
+    vec_ref[...] = total
+    total = sum_z(0)
+    for j in range(3):
+        gmix_ref[j] = total[:, j * TILE : (j + 1) * TILE]
+    for copy in started:
+        copy.wait_send()
+    assert len(started) == copies
+
+
+def local(sizes, *arrays):
+    n = sizes["dp"]
+    inputs, mixing, up = arrays[0], arrays[2], arrays[4]
+    shard = mixing.shape[1]
+    fits = (
+        shard % 16 == 0
+        and n % (X * C) == 0
+        and sizes["tensor"] == 2
+        and inputs.shape == (SEQ, 768)
+        and mixing.shape[2] == TILE
+        and up.shape[1] == 1536
+    )
+    if not fits:
+        return local_plain(*arrays)
+    (
+        inputs,
+        cotangent,
+        mixing,
+        output,
+        up,
+        down,
+        first_gain,
+        first_shift,
+        attend_bias,
+        output_bias,
+        hidden_bias,
+        final_bias,
+        second_gain,
+        second_shift,
+    ) = arrays
+    Z = n // (X * C)
+    width = inputs.shape[1]
+    sizes_of = (3 * TILE, TILE, up.shape[1], up.shape[1])
+    pad = ((0, ROWS - SEQ), (0, 0))
+    copies = 4 * (Z - 1 + 3 * Z) + 4 + 4 * (Z + 1) + Z + 1
+    vmem = pl.BlockSpec(memory_space=pltpu.VMEM)
+    full = [pltpu.VMEM((Z, X, C, shard, k), BF16) for k in sizes_of]
+    half = [pltpu.VMEM((Z, X, shard, k), BF16) for k in sizes_of]
+    quarter = [pltpu.VMEM((Z, shard, k), BF16) for k in sizes_of]
+    outs = pl.pallas_call(
+        functools.partial(layer_kernel, Z, copies),
+        out_shape=(
+            jax.ShapeDtypeStruct((ROWS, width), BF16),
+            jax.ShapeDtypeStruct((ROWS, width), BF16),
+            jax.ShapeDtypeStruct((3, shard, TILE), F32),
+            jax.ShapeDtypeStruct((shard, TILE), F32),
+            jax.ShapeDtypeStruct((shard, up.shape[1]), F32),
+            jax.ShapeDtypeStruct((shard, up.shape[1]), F32),
+            jax.ShapeDtypeStruct((16, width), F32),
+        ),
+        in_specs=[vmem] * 14,
+        out_specs=(vmem,) * 7,
+        scratch_shapes=full
+        + full
+        + half
+        + half
+        + quarter
+        + quarter
+        + quarter
+        + [
+            pltpu.VMEM((4, ROWS, width), BF16),
+            pltpu.VMEM((4, ROWS, width), BF16),
+            pltpu.VMEM((16, width), F32),
+            pltpu.VMEM((3 + Z, 16, width), F32),
+            pltpu.VMEM((3, width, ROWS), BF16),
+            pltpu.VMEM((ROWS, width), F32),
+            pltpu.VMEM((ROWS, width), F32),
+            pltpu.VMEM((ROWS, width), F32),
+            pltpu.VMEM((ROWS, 3 * TILE), BF16),
+            pltpu.VMEM((TILE // HD, ROWS, ROWS), F32),
+            pltpu.VMEM((ROWS, TILE), BF16),
+            pltpu.VMEM((ROWS, TILE), BF16),
+            pltpu.VMEM((ROWS, 3 * TILE), BF16),
+            pltpu.VMEM((ROWS, up.shape[1]), BF16),
+            pltpu.VMEM((ROWS, up.shape[1]), F32),
+            pltpu.VMEM((ROWS, up.shape[1]), BF16),
+            pltpu.VMEM((ROWS, width), BF16),
+            pltpu.VMEM((ROWS, width), F32),
+            pltpu.VMEM((ROWS, width), F32),
+            pltpu.SemaphoreType.DMA((copies,)),
+            pltpu.SemaphoreType.DMA((copies,)),
+        ],
+        compiler_params=pltpu.CompilerParams(
+            collective_id=0, has_side_effects=True, vmem_limit_bytes=60 * 1024 * 1024
+        ),
+    )(
+        jnp.pad(inputs, pad),
+        jnp.pad(cotangent, pad),
+        mixing,
+        output.T,
+        up,
+        down.T,
+        first_gain.reshape(1, -1),
+        first_shift.reshape(1, -1),
+        attend_bias,
+        output_bias.reshape(1, -1),
+        hidden_bias.reshape(1, -1),
+        final_bias.reshape(1, -1),
+        second_gain.reshape(1, -1),
+        second_shift.reshape(1, -1),
+    )
+    layer_output, input_grad, gmix, gout, gup, gdown, vec = outs
+    return (
+        layer_output[:SEQ],
+        input_grad[:SEQ],
+        gmix,
+        gout.T,
+        gup,
+        gdown.T,
+        vec[0],
+        vec[1],
+        vec[2].reshape(2, TILE),
+        vec[3],
+        vec[4:6].reshape(-1),
+        vec[6],
+        vec[7],
+        vec[8],
+    )
+
+
 def solution(mesh):
     placed = (
         P("dp", None),
@@ -189,7 +707,7 @@
         P(),
     )
     return jax.shard_map(
-        local,
+        functools.partial(local, dict(mesh.shape)),
         mesh=mesh,
         in_specs=placed,
         out_specs=(

time: 628 us -> 141 us (0.22)
  waiting for transfers between devices: 453 us -> 0 us
  Pallas kernels: 0 us -> 124 us
  blocking collectives: 89.2 us -> 0 us
  matrix products: 40.8 us -> 0 us
  between operations: 15.3 us -> 0.7 us
  other arithmetic: 11 us -> 0 us
    reduce_scatter x3 -> x0, waiting for transfers between devices: 219 us -> none  [the longest x1 79.5 us: local(): lax.psum_scatter(up_grad, 'dp', scatter_dimension=0, tiled=True)]
    pallas_call x0 -> x1, Pallas kernels: none -> 124 us  [local(): pl.pallas_call(functools.partial(layer_kernel, Z, copies), out_shape=(jax...]
    all_gather x3 -> x0, waiting for transfers between devices: 99.5 us -> none  [the longest x1 42.2 us: local(): lax.all_gather(up_weight, 'dp', axis=0, tiled=True)]
    psum x3 -> x0, waiting for transfers between devices: 78 us -> none  [the longest x1 28.3 us: local(): lax.psum(matmul(attended, output_full), 'tensor')]
    psum x1 -> x0, blocking collectives: 63.5 us -> none  [local(): lax.psum((firstgain_grad, firstshift_grad, attendbias_grad, outbias_grad,...]
    unnamed x11 -> x0, waiting for transfers between devices: 56.7 us -> none
    dot_general x18 -> x0, matrix products: 40.8 us -> none  [the longest x9 22.2 us: matmul(): return jnp.dot(left, right, preferred_element_type=jnp.float32)]
    all_gather x1 -> x0, blocking collectives: 25.7 us -> none  [local(): lax.all_gather(output_weight, 'dp', axis=1, tiled=True)]
  transfers between devices with their start and end apart: 10 -> 0, of which waited for: 10 -> 0; matrix products, arithmetic and copies ran while one was open for 6% -> 0% of each run, Pallas kernels for 0% -> 0%
where the time goes in v1:
time: 141 us
  Pallas kernels  124 us (88%)
  local copies, waits for them, and re-layouts  15.7 us (11%)
    pallas_call x1, Pallas kernels, local(): pl.pallas_call(functools.partial(layer_kernel, Z, copies), out_shape=(jax...  124 us
    unnamed x30, local copies, waits for them, and re-layouts  3.98 us

profile of v1, /device:TPU:0, one launch (start us, length us, event | category | flops | bytes accessed | tf_op | source)
XLA Modules:
  0.0 140.8 jit_solution(2028947263044210536)
XLA Ops:
  0.6 0.0 copy-start.8
  0.7 1.3 reshape.52.fg_ref
  1.9 0.0 copy-done.8
  1.9 0.0 copy-start.9
  1.9 0.6 reshape.53.fs_ref
  2.5 0.1 copy-done.9
  2.6 0.0 copy-start.10
  2.6 0.6 reshape.54.ob_ref
  3.2 0.1 copy-done.10
  3.3 0.0 copy-start.11
  3.3 0.0 copy-start.12
  3.3 0.6 reshape.56.fb_ref
  3.9 0.1 copy-done.11
  4.0 0.0 copy-start.7
  4.0 0.6 reshape.57.sg_ref
  4.6 0.0 copy-done.12
  4.6 0.6 reshape.58.ss_ref
  5.2 0.0 copy-done.7
  5.2 0.6 reshape.55.hb_ref
  5.8 0.0 copy-start
  5.8 1.8 %pad.7.x_ref = bf16[256,768]{1,0:T(8,128)(2,1)} pad(bf16[197,768]{1,0:T(8,128)(2,1)} %param.14, bf16[]{:T(256)} %constant.2.clone.1), padding=0_59x0_0 | pad | bytes 695810 | tf_op jit(solution)/shard_map/jit(_pad)/pad | solution.py:658
  7.5 0.0 copy-done
  7.5 0.8 pad.8.ct_ref
  8.3 124.5 %shard_map.245 = (bf16[256,768]{1,0:T(8,128)(2,1)}, bf16[256,768]{1,0:T(8,128)(2,1)}, f32[3,48,384]{2,1,0:T(8,128)}, f32[48,384]{1,0:T(8,128)}, f32[48,1536]{1,0...) custom-call(bf16[256,768]{1,0:T(8,128)(2,1)} %pad.7.x_ref, bf16[256,768]{1,0:T(8,128)(2,1)} %pad.8.ct_ref, ...), custom_call_target="tpu_custom_call" | custom-call | tf_op jit(solution)/shard_map/pallas_call | solution.py:611
  132.8 0.0 copy-start.3
  132.8 0.0 copy-start.6
  132.8 1.8 %slice.30 = bf16[197,768]{1,0:T(8,128)(2,1)} slice(bf16[256,768]{1,0:T(8,128)(2,1)} %get-tuple-element.21), slice={[0:197], [0:768]} | slice | bytes 605184 | tf_op jit(solution)/shard_map/slice | solution.py:675
  134.6 0.0 copy-done.6
  134.6 0.7 slice_reduce_fusion
  135.2 0.6 reshape.59
  135.8 0.6 reshape_squeeze.3
  136.4 0.0 copy-done.3
  136.4 0.0 copy-start.4
  136.4 0.7 slice.31
  137.2 0.3 copy-done.4
  137.5 0.0 copy-start.5
  137.5 0.0 copy-start.2
  137.5 0.7 copy.32
  138.2 0.2 copy-done.5
  138.4 0.6 copy.33
  139.0 0.0 copy-done.2
  139.0 0.0 copy-start.1
  139.0 0.7 copy.34
  139.7 0.4 copy-done.1
  140.1 0.7 copy.35
  (1 shorter events, 0.0 us)
Async XLA Ops:
  0.6 1.3 copy-start.8
  1.9 0.7 copy-start.9
  2.6 0.7 copy-start.10
  3.3 0.7 copy-start.11
  3.3 1.3 copy-start.12
  4.0 1.2 copy-start.7
  5.8 1.8 %copy-start = (bf16[197,768]{1,0:T(8,128)(2,1)S(1)}, bf16[197,768]{1,0:T(8,128)(2,1)}, u32[]{:S(2)}) copy-start(bf16[197,768]{1,0:T(8,128)(2,1)} %param.15) | copy-start | bytes 907780
  132.8 3.6 %copy-start.3 = (bf16[256,768]{1,0:T(8,128)(2,1)S(1)}, bf16[256,768]{1,0:T(8,128)(2,1)}, u32[]{:S(2)}) copy-start(bf16[256,768]{1,0:T(8,128)(2,1)} %get-tuple-element.22) | copy-start | bytes 1179652
  132.8 1.8 %copy-start.6 = (f32[16,768]{1,0:T(8,128)S(1)}, f32[16,768]{1,0:T(8,128)}, u32[]{:S(2)}) copy-start(f32[16,768]{1,0:T(8,128)} %get-tuple-element.27) | copy-start | bytes 147460
  136.4 1.0 copy-start.4
  137.5 0.9 copy-start.5
  137.5 1.5 %copy-start.2 = (f32[48,1536]{1,0:T(8,128)S(1)}, f32[48,1536]{1,0:T(8,128)}, u32[]{:S(2)}) copy-start(f32[48,1536]{1,0:T(8,128)} %get-tuple-element.53) | copy-start | bytes 884740
  139.0 1.1 copy-start.1

commit v2 on v1

--- a/solution.py
+++ b/solution.py
@@ -268,6 +268,8 @@
     a2_s,
     res_s,
     rg_s,
+    ct_s,
+    rows_s,
     send_sem,
     recv_sem,
 ):
@@ -325,12 +327,16 @@
     pl.semaphore_wait(barrier, len(everyone))
 
     by_z, by_x, by_c, by_d = {}, {}, {}, {}
-    for i in range(4):
+
+    def own(i):
         mine = w[i].at[z, x, c]
         by_x[i, 0] = send(mine, mine, peer_x)
         for d in range(1, Z):
             by_z[i, d] = send(mine, mine, peers_z[d - 1])
         by_c[i, 0] = send(mine, mine, peer_c)
+
+    own(0)
+    own(1)
 
     def pass_on(i):
         for d in range(1, Z):
@@ -363,17 +369,30 @@
     def transposed(value):
         return value.astype(F32).T.astype(BF16)
 
-    source = x_ref[...].astype(F32)
-    n1, r1, affine = norm_forward(source, fg_ref[...], fs_ref[...])
+    rg_s[192:ROWS, :] = jnp.zeros((ROWS - 192, rg_s.shape[1]), F32)
+    rg_s[0:SEQ, :] = x_ref[...].astype(F32)
+    acc[192:ROWS, :] = jnp.zeros((ROWS - 192, acc.shape[1]), F32)
+    acc[0:SEQ, :] = ct_ref[...].astype(F32)
+    ct_s[...] = acc[...].astype(BF16)
+    for row, ref in enumerate((fg_ref, fs_ref, ob_ref, fb_ref, sg_ref)):
+        rows_s[row : row + 1, 0:768] = ref[...].reshape(1, -1)
+    rows_s[0:1, 768:1536] = ss_ref[...].reshape(1, -1)
+    rows_s[5:6, :] = hb_ref[...].reshape(1, -1)
+    fg_row, fs_row, ob_row, fb_row, sg_row = (rows_s.at[r : r + 1, 0:768] for r in range(5))
+    ss_row = rows_s.at[0:1, 768:1536]
+    source = rg_s[...]
+    n1, r1, affine = norm_forward(source, fg_row[...], fs_row[...])
     n1_s[...] = n1
     a1 = affine.astype(BF16)
     left_t[0] = transposed(a1)
-    left_t[1] = transposed(ct_ref[...])
+    left_t[1] = transposed(ct_s[...])
     vs[...] = jnp.zeros_like(vs)
-    vs[6:7, :] = jnp.sum(ct_ref[...].astype(F32), axis=0, keepdims=True)
+    vs[6:7, :] = jnp.sum(ct_s[...].astype(F32), axis=0, keepdims=True)
     pass_on(0)
+    own(2)
     pass_core(0)
     pass_on(1)
+    own(3)
     gathered(0)
 
     for j in range(3):
@@ -411,24 +430,54 @@
     pass_core(2)
     pass_on(3)
     first.wait_recv()
-    residual = source + exchanged(0) + ob_ref[...]
+    residual = source + exchanged(0) + ob_row[...]
     res_s[...] = residual
-    n2, r2, affine = norm_forward(residual, sg_ref[...], ss_ref[...])
+    n2, r2, affine = norm_forward(residual, sg_row[...], ss_row[...])
     n2_s[...] = n2
     a2_s[...] = affine.astype(BF16)
     left_t[2] = transposed(affine.astype(BF16))
     gathered(2)
-    tiles = hb_ref.shape[1] // TILE
+    tiles = hb_ref.shape[0] // TILE
 
     def hidden(tile, carry):
         value = jnp.dot(a2_s[...], weight(2, tile), preferred_element_type=F32)
-        value, steep = gelu_pair(value + hb_ref[:, cols(tile)])
+        value, steep = gelu_pair(value + rows_s[5:6, cols(tile)])
         active[:, cols(tile)] = value.astype(BF16)
         slope[:, cols(tile)] = steep
         return carry
 
     lax.fori_loop(0, tiles, hidden, 0)
     pass_core(3)
+    by_a, by_b, by_e = {}, {}, {}
+
+    def gradient(i, left, right, count):
+        def one(tile, carry):
+            value = jnp.dot(left_t[left], right[:, cols(tile)], preferred_element_type=F32)
+            g[i][:, :, :, :, cols(tile)] = value.astype(BF16).reshape(Z, X, C, -1, TILE)
+            return carry
+
+        lax.fori_loop(0, count, one, 0)
+        by_a[i] = send(g[i].at[:, :, 1 - c], ga[i], peer_c)
+
+    def sum_core(i):
+        by_a[i].wait_recv()
+        gb[i][...] = (g[i][:, :, c].astype(F32) + ga[i][...].astype(F32)).astype(BF16)
+        by_b[i] = send(gb[i].at[:, 1 - x], gc[i], peer_x)
+
+    def sum_x(i):
+        by_b[i].wait_recv()
+        gd[i][...] = (gb[i][:, x].astype(F32) + gc[i][...].astype(F32)).astype(BF16)
+        for d in range(1, Z):
+            by_e[i, d] = send(gd[i].at[zat(d)], ge[i].at[d], peers_z[d - 1])
+
+    def sum_z(i):
+        total = gd[i][z].astype(F32)
+        for d in range(1, Z):
+            by_e[i, d].wait_recv()
+            total = total + ge[i][d].astype(F32)
+        return total
+
+    gradient(3, 1, active, tiles)
     gathered(3)
 
     acc[...] = jnp.zeros_like(acc)
@@ -440,11 +489,12 @@
     lax.fori_loop(0, tiles, second, 0)
     ysend[1] = acc[...].astype(BF16)
     out_copy = exchange(1)
+    sum_core(3)
 
     acc[...] = jnp.zeros_like(acc)
 
     def back(tile, carry):
-        grad = jnp.dot(ct_ref[...], weight(3, tile), preferred_element_type=F32)
+        grad = jnp.dot(ct_s[...], weight(3, tile), preferred_element_type=F32)
         grad = grad * slope[:, cols(tile)]
         sums = jnp.sum(grad, axis=0, keepdims=True)
         slope[0:8, cols(tile)] = jnp.broadcast_to(sums, (8, TILE))
@@ -459,53 +509,22 @@
     vs[4:5, :] = slope[0:1, 0:768]
     vs[5:6, :] = slope[0:1, 768:1536]
 
-    by_a, by_b, by_e = {}, {}, {}
-
-    def gradient(i, left, right, count):
-        def one(tile, carry):
-            value = jnp.dot(left_t[left], right[:, cols(tile)], preferred_element_type=F32)
-            g[i][:, :, :, :, cols(tile)] = value.astype(BF16).reshape(Z, X, C, -1, TILE)
-            return carry
-
-        lax.fori_loop(0, count, one, 0)
-        by_a[i] = send(g[i].at[:, :, 1 - c], ga[i], peer_c)
-
-    def sum_core(i):
-        by_a[i].wait_recv()
-        gb[i][...] = (g[i][:, :, c].astype(F32) + ga[i][...].astype(F32)).astype(BF16)
-        by_b[i] = send(gb[i].at[:, 1 - x], gc[i], peer_x)
-
-    def sum_x(i):
-        by_b[i].wait_recv()
-        gd[i][...] = (gb[i][:, x].astype(F32) + gc[i][...].astype(F32)).astype(BF16)
-        for d in range(1, Z):
-            by_e[i, d] = send(gd[i].at[zat(d)], ge[i].at[d], peers_z[d - 1])
-
-    def sum_z(i):
-        total = gd[i][z].astype(F32)
-        for d in range(1, Z):
-            by_e[i, d].wait_recv()
-            total = total + ge[i][d].astype(F32)
-        return total
-
-    gradient(3, 1, active, tiles)
     gradient(2, 2, pre_half, tiles)
-    sum_core(3)
     out_copy.wait_recv()
-    lo_ref[...] = (res_s[...] + exchanged(1) + fb_ref[...]).astype(BF16)
+    lo_ref[...] = (res_s[...] + exchanged(1) + fb_row[...]).astype(BF16)
     a2_copy.wait_recv()
     a2_grad = exchanged(2)
     vs[7:8, :] = jnp.sum(a2_grad * n2_s[...], axis=0, keepdims=True)
     vs[8:9, :] = jnp.sum(a2_grad, axis=0, keepdims=True)
-    res_grad = ct_ref[...].astype(F32) + norm_backward(a2_grad, n2_s[...], r2, sg_ref[...])
+    res_grad = ct_s[...].astype(F32) + norm_backward(a2_grad, n2_s[...], r2, sg_row[...])
     rg_s[...] = res_grad
     vs[3:4, :] = jnp.sum(res_grad, axis=0, keepdims=True)
     res_half = res_grad.astype(BF16)
     left_t[1] = transposed(res_half)
     sum_core(2)
+    sum_x(3)
     attg[...] = jnp.dot(res_half, weight(1, 0), preferred_element_type=F32).astype(BF16)
     gradient(1, 1, att, 1)
-    sum_x(3)
 
     pairs = {}
     for h in range(heads):
@@ -543,7 +562,7 @@
     vs[1:2, :] = jnp.sum(a1_grad, axis=0, keepdims=True)
     vec_c = send(vs, vr.at[0], peer_c)
     sum_core(0)
-    ig_ref[...] = (rg_s[...] + norm_backward(a1_grad, n1_s[...], r1, fg_ref[...])).astype(BF16)
+    ig_ref[...] = (rg_s[...] + norm_backward(a1_grad, n1_s[...], r1, fg_row[...])).astype(BF16)
     vec_c.wait_recv()
     vr[1] = vs[...] + vr[0]
     vec_x = send(vr.at[1], vr.at[2], peer_x)
@@ -602,7 +621,6 @@
     Z = n // (X * C)
     width = inputs.shape[1]
     sizes_of = (3 * TILE, TILE, up.shape[1], up.shape[1])
-    pad = ((0, ROWS - SEQ), (0, 0))
     copies = 4 * (Z - 1 + 3 * Z) + 4 + 4 * (Z + 1) + Z + 1
     vmem = pl.BlockSpec(memory_space=pltpu.VMEM)
     full = [pltpu.VMEM((Z, X, C, shard, k), BF16) for k in sizes_of]
@@ -648,6 +666,8 @@
             pltpu.VMEM((ROWS, width), BF16),
             pltpu.VMEM((ROWS, width), F32),
             pltpu.VMEM((ROWS, width), F32),
+            pltpu.VMEM((ROWS, width), BF16),
+            pltpu.VMEM((6, up.shape[1]), F32),
             pltpu.SemaphoreType.DMA((copies,)),
             pltpu.SemaphoreType.DMA((copies,)),
         ],
@@ -655,20 +675,20 @@
             collective_id=0, has_side_effects=True, vmem_limit_bytes=60 * 1024 * 1024
         ),
     )(
-        jnp.pad(inputs, pad),
-        jnp.pad(cotangent, pad),
+        inputs,
+        cotangent,
         mixing,
         output.T,
         up,
         down.T,
-        first_gain.reshape(1, -1),
-        first_shift.reshape(1, -1),
+        first_gain,
+        first_shift,
         attend_bias,
-        output_bias.reshape(1, -1),
-        hidden_bias.reshape(1, -1),
-        final_bias.reshape(1, -1),
-        second_gain.reshape(1, -1),
-        second_shift.reshape(1, -1),
+        output_bias,
+        hidden_bias,
+        final_bias,
+        second_gain,
+        second_shift,
     )
     layer_output, input_grad, gmix, gout, gup, gdown, vec = outs
     return (

time: 141 us -> 135 us (0.957)
  local copies, waits for them, and re-layouts: 15.7 us -> 9.77 us
    reshape x7 -> x0, local copies, waits for them, and re-layouts: 4.77 us -> none  [the longest x1 1.27 us: local(): first_gain.reshape(1, -1)]
    pad x2 -> x0, local copies, waits for them, and re-layouts: 2.55 us -> none  [the longest x1 1.77 us: local(): jnp.pad(inputs, pad)]
    unnamed x30 -> x14, local copies, waits for them, and re-layouts: 3.98 us -> 3.63 us
where the time goes in v2:
time: 135 us
  Pallas kernels  124 us (92%)
  local copies, waits for them, and re-layouts  9.77 us (7%)
    pallas_call x1, Pallas kernels, local(): pl.pallas_call(functools.partial(layer_kernel, Z, copies), out_shape=(jax...  124 us
    unnamed x14, local copies, waits for them, and re-layouts  3.63 us

profile of v2, /device:TPU:0, one launch (start us, length us, event | category | flops | bytes accessed | tf_op | source)
XLA Modules:
  0.0 134.6 jit_solution(1878753894441857424)
XLA Ops:
  0.7 124.2 %shard_map.245 = (bf16[256,768]{1,0:T(8,128)(2,1)}, bf16[256,768]{1,0:T(8,128)(2,1)}, f32[3,48,384]{2,1,0:T(8,128)}, f32[48,384]{1,0:T(8,128)}, f32[48,1536]{1,0...) custom-call(bf16[197,768]{1,0:T(8,128)(2,1)} %x_ref.1, bf16[197,768]{1,0:T(8,128)(2,1)} %ct_ref.1, ...), custom_call_target="tpu_custom_call" | custom-call | tf_op jit(solution)/shard_map/pallas_call | solution.py:629
  124.8 0.0 copy-start.2
  124.9 1.8 %slice_reduce_fusion = (f32[768]{0:T(1024)}, f32[768]{0:T(1024)}, f32[768]{0:T(1024)}, f32[768]{0:T(1024)}, f32[768]{0:T(1024)S(1)}, /*index=5*/f32[768]{0:T(1024)}, f32[768]{0:T(1024)}) fusion(f32[16,768]{1,0:T(8,128)} %get-tuple-element.27), kind=kLoop, calls=%fused_computation | loop fusion | bytes 43008 | tf_op jit(solution)/shard_map/slice | solution.py:708
  126.6 0.6 reshape_squeeze.3
  127.2 0.7 slice.36
  127.9 0.6 reshape.31
  128.5 1.7 %slice.30 = bf16[197,768]{1,0:T(8,128)(2,1)} slice(bf16[256,768]{1,0:T(8,128)(2,1)} %get-tuple-element.21), slice={[0:197], [0:768]} | slice | bytes 605184 | tf_op jit(solution)/shard_map/slice | solution.py:695
  130.3 0.0 copy-done.2
  130.3 0.0 copy-start.3
  130.3 0.7 slice.31
  131.0 0.3 copy-done.3
  131.3 0.0 copy-start.4
  131.3 0.0 copy-start.1
  131.3 0.7 copy.32
  132.0 0.2 copy-done.4
  132.2 0.6 copy.33
  132.8 0.0 copy-done.1
  132.8 0.0 copy-start
  132.8 0.7 copy.34
  133.6 0.4 copy-done
  133.9 0.7 copy.35
Async XLA Ops:
  124.8 5.4 %copy-start.2 = (bf16[256,768]{1,0:T(8,128)(2,1)S(1)}, bf16[256,768]{1,0:T(8,128)(2,1)}, u32[]{:S(2)}) copy-start(bf16[256,768]{1,0:T(8,128)(2,1)} %get-tuple-element.22) | copy-start | bytes 1179652
  130.3 1.0 copy-start.3
  131.3 0.9 copy-start.4
  131.3 1.5 %copy-start.1 = (f32[48,1536]{1,0:T(8,128)S(1)}, f32[48,1536]{1,0:T(8,128)}, u32[]{:S(2)}) copy-start(f32[48,1536]{1,0:T(8,128)} %get-tuple-element.53) | copy-start | bytes 884740
  132.8 1.1 copy-start

commit v3 on v2

--- a/solution.py
+++ b/solution.py
@@ -549,19 +549,19 @@
             sum_core(1)
         if h == 3:
             sum_x(2)
+    gradient(0, 0, stacked, 3)
     total = nt(stacked[:, 0:TILE], weight(0, 0))
     for j in range(1, 3):
         total = total + nt(stacked[:, j * TILE : (j + 1) * TILE], weight(0, j))
     ysend[3] = total.astype(BF16)
     last = exchange(3)
-    gradient(0, 0, stacked, 3)
+    sum_core(0)
     sum_x(1)
     last.wait_recv()
     a1_grad = exchanged(3)
     vs[0:1, :] = jnp.sum(a1_grad * n1_s[...], axis=0, keepdims=True)
     vs[1:2, :] = jnp.sum(a1_grad, axis=0, keepdims=True)
     vec_c = send(vs, vr.at[0], peer_c)
-    sum_core(0)
     ig_ref[...] = (rg_s[...] + norm_backward(a1_grad, n1_s[...], r1, fg_row[...])).astype(BF16)
     vec_c.wait_recv()
     vr[1] = vs[...] + vr[0]

time: 135 us -> 133 us (0.985)
  Pallas kernels: 124 us -> 122 us
    pallas_call x1, Pallas kernels: 124 us -> 122 us  [local(): pl.pallas_call(functools.partial(layer_kernel, Z, copies), out_shape=(jax...]
where the time goes in v3:
time: 133 us
  Pallas kernels  122 us (92%)
  local copies, waits for them, and re-layouts  9.77 us (7%)
    pallas_call x1, Pallas kernels, local(): pl.pallas_call(functools.partial(layer_kernel, Z, copies), out_shape=(jax...  122 us
    unnamed x14, local copies, waits for them, and re-layouts  3.63 us

profile of v3, /device:TPU:0, one launch (start us, length us, event | category | flops | bytes accessed | tf_op | source)
XLA Modules:
  0.0 132.7 jit_solution(15511533207700630062)
XLA Ops:
  0.7 122.3 %shard_map.245 = (bf16[256,768]{1,0:T(8,128)(2,1)}, bf16[256,768]{1,0:T(8,128)(2,1)}, f32[3,48,384]{2,1,0:T(8,128)}, f32[48,384]{1,0:T(8,128)}, f32[48,1536]{1,0...) custom-call(bf16[197,768]{1,0:T(8,128)(2,1)} %x_ref.1, bf16[197,768]{1,0:T(8,128)(2,1)} %ct_ref.1, ...), custom_call_target="tpu_custom_call" | custom-call | tf_op jit(solution)/shard_map/pallas_call | solution.py:629
  122.9 0.0 copy-start.2
  122.9 1.8 %slice_reduce_fusion = (f32[768]{0:T(1024)}, f32[768]{0:T(1024)}, f32[768]{0:T(1024)}, f32[768]{0:T(1024)}, f32[768]{0:T(1024)S(1)}, /*index=5*/f32[768]{0:T(1024)}, f32[768]{0:T(1024)}) fusion(f32[16,768]{1,0:T(8,128)} %get-tuple-element.27), kind=kLoop, calls=%fused_computation | loop fusion | bytes 43008 | tf_op jit(solution)/shard_map/slice | solution.py:708
  124.7 0.6 reshape_squeeze.3
  125.3 0.7 slice.36
  126.0 0.6 reshape.31
  126.6 1.7 %slice.30 = bf16[197,768]{1,0:T(8,128)(2,1)} slice(bf16[256,768]{1,0:T(8,128)(2,1)} %get-tuple-element.21), slice={[0:197], [0:768]} | slice | bytes 605184 | tf_op jit(solution)/shard_map/slice | solution.py:695
  128.3 0.0 copy-done.2
  128.3 0.0 copy-start.3
  128.3 0.7 slice.31
  129.1 0.3 copy-done.3
  129.4 0.0 copy-start.4
  129.4 0.0 copy-start.1
  129.4 0.7 copy.32
  130.1 0.2 copy-done.4
  130.3 0.6 copy.33
  130.9 0.0 copy-done.1
  130.9 0.0 copy-start
  130.9 0.7 copy.34
  131.6 0.4 copy-done
  132.0 0.7 copy.35
Async XLA Ops:
  122.9 5.4 %copy-start.2 = (bf16[256,768]{1,0:T(8,128)(2,1)S(1)}, bf16[256,768]{1,0:T(8,128)(2,1)}, u32[]{:S(2)}) copy-start(bf16[256,768]{1,0:T(8,128)(2,1)} %get-tuple-element.22) | copy-start | bytes 1179652
  128.3 1.0 copy-start.3
  129.4 0.9 copy-start.4
  129.4 1.5 %copy-start.1 = (f32[48,1536]{1,0:T(8,128)S(1)}, f32[48,1536]{1,0:T(8,128)}, u32[]{:S(2)}) copy-start(f32[48,1536]{1,0:T(8,128)} %get-tuple-element.53) | copy-start | bytes 884740
  130.9 1.1 copy-start
